TPU v7x, 128 devices: a whole 4x4x4 slice. The times are simulated.
128 devices in a mesh: depth: 2 (over core), rows: 2 (over x_hi), shots: 32 (over z, y, x_lo).
Axes of the slice: x: 4 (x_hi: 2, x_lo: 2; x = x_hi * 2 + x_lo), y: 4, z: 4, core: 2. Of those that a mesh axis runs over, the one named last changes fastest.
Arguments:
- sources: float32 [2, 2, 1024, 4096], P('depth', None, 'rows', 'shots'), may hold values from -6 to 6
- factor: float32 [2, 2, 1024, 1024], P('depth', None, ('rows', 'shots')), may hold values from -0.09375 to 0.09375
- block_mask: int32 [2, 2, 8, 8], P('depth'), may hold values 0 or 1
- inverse_diagonal: float32 [2, 2, 1024, 1024], P('depth', None, None, 'rows'), may hold values from -1.2 to 1.2, as said below
Outputs:
- solution: float32 [2, 2, 1024, 4096], P('depth', None, 'rows', 'shots')
Inputs may be any that keep to these rules, and one draw needn't show every extreme that they name: Each block inverse_diagonal[d, m] is lower triangular with diagonal entries between 0.8 and 1.2.
All inputs are finite; a program needn't handle non-finite values. No bound on the sum of `block_mask` on one device may be relied on, other than what follows from the above.
Results may differ from a plain program's by a relative error of at most 0.0001.
Values sent between devices are 32-bit elements; how exact they have to be, the bound alone decides.
A program may use at most 64 MiB of HBM per device.

v0:
```python
import jax
import jax.numpy as jnp
from jax import lax
from jax.sharding import PartitionSpec as P


def mask_rows(factor_rows, block_mask, row_start, block_size):
    row_total = factor_rows.shape[1]
    block_count = block_mask.shape[3]
    row_blocks = (row_start + jnp.arange(row_total, dtype=jnp.int32)) // block_size
    row_select = (row_blocks[:, None] == jnp.arange(block_count, dtype=jnp.int32)[None, :]).astype(
        jnp.float32
    )
    row_masks = jnp.einsum("rk,pkc->prc", row_select, block_mask[0].astype(jnp.float32))
    return factor_rows * jnp.repeat(row_masks, block_size, axis=2)


def group_reduce(partial_value):
    summed = lax.psum_scatter(partial_value, "depth", scatter_dimension=0, tiled=True)
    return summed[0]


def group_collect(spread):
    every_rows = lax.all_gather(spread[None], "depth", axis=0, tiled=True)
    return every_rows


def invert_level(inverse_block, own_rows):
    inverse_term = jnp.dot(
        inverse_block, own_rows, precision=lax.Precision.HIGHEST, preferred_element_type=jnp.float32
    )
    return lax.psum(inverse_term, "rows")


def per_device(sources, factor, block_mask, inverse_diagonal):
    depth_count = lax.axis_size("depth")
    tree_height = depth_count.bit_length() - 1
    level_count = tree_height + 1
    shot_index = lax.axis_index("shots")
    rows_index = lax.axis_index("rows")
    thin_rows = factor.shape[2]
    full_width = factor.shape[3]
    block_count = block_mask.shape[3]
    block_size = full_width // block_count
    highest = lax.Precision.HIGHEST
    row_start = (rows_index * lax.axis_size("shots") + shot_index) * thin_rows
    masked = mask_rows(factor[0], block_mask, row_start, block_size)
    solved = []
    wide_solved = []
    for tier_index in range(level_count):
        own_rows = sources[0, tier_index]
        if tier_index > 0:
            group_size = 2**tier_index
            factor_tiles = masked.reshape(tier_index, group_size, thin_rows, full_width)
            lower_solved = jnp.stack(wide_solved[:tier_index])
            partial_value = jnp.einsum(
                "lgrs,lsn->grn",
                factor_tiles,
                lower_solved,
                precision=highest,
                preferred_element_type=jnp.float32,
            )
            reduced = group_reduce(partial_value)
            reduced = lax.all_to_all(reduced, "shots", split_axis=1, concat_axis=0, tiled=True)
            own_rows = own_rows - reduced
        full_rows = invert_level(inverse_diagonal[0, tier_index], own_rows)
        solved.append(full_rows)
        if tier_index < tree_height:
            wide_solved.append(lax.all_gather(full_rows, "shots", axis=1, tiled=True))
    answers = [None] * level_count
    collected = {}
    for tier_index in reversed(range(level_count)):
        target = solved[tier_index]
        if tier_index < tree_height:
            factor_tiles = masked
            transposed = jnp.einsum(
                "grs,grn->sn",
                factor_tiles,
                collected[1],
                precision=highest,
                preferred_element_type=jnp.float32,
            )
            shot_piece = lax.psum_scatter(transposed, "shots", scatter_dimension=1, tiled=True)
            own_columns = lax.psum(shot_piece, "rows")
            target = target - own_columns
        answer = lax.dot_general(
            inverse_diagonal[0, tier_index],
            target,
            (((0,), (0,)), ((), ())),
            precision=highest,
            preferred_element_type=jnp.float32,
        )
        answers[tier_index] = answer
        if tier_index > 0:
            spread = lax.all_to_all(answer, "shots", split_axis=0, concat_axis=1, tiled=True)
            collected[tier_index] = group_collect(spread)
    return jnp.stack(answers)[None]


def solution(mesh):
    placed = (
        P("depth", None, "rows", "shots"),
        P("depth", None, ("rows", "shots"), None),
        P("depth", None, None, None),
        P("depth", None, None, "rows"),
    )
    return jax.shard_map(
        per_device,
        mesh=mesh,
        in_specs=placed,
        out_specs=P("depth", None, "rows", "shots"),
        check_vma=False,
    )
```

profile of v0, /device:TPU:1, one launch (start us, length us, event | category | flops | bytes accessed | tf_op | source)
XLA Modules:
  0.0 942.0 jit_solution(3403991604582665466)
XLA Ops:
  6.5 0.0 copy-start.1
  6.5 0.0 all-reduce.4.cloned.1.call-start
  6.5 4.2 fusion.8
  10.8 0.0 all-reduce.4.cloned.1.call-update
  10.8 0.0 all-gather.2.cloned.1.call-start
  10.8 40.0 %all-reduce.4.cloned.1.call-done = f32[1024,128]{1,0:T(8,128)} async-done(((f32[1024,128]{1,0:T(8,128)}), f32[1024,128]{1,0:T(8,128)}) %all-reduce.4.cloned.1.call-update) | async-done | bytes 524304 | tf_op jit(solution)/shard_map/psum | solution.py:32
  50.8 0.0 all-gather.2.cloned.1.call-update
  50.8 0.0 reduce-scatter.3.cloned.1.call-start
  50.9 0.7 convert_bitcast_fusion
  51.6 0.1 copy.15
  51.7 0.1 convolution_bitcast_fusion.1
  51.8 0.1 copy.16
  51.9 0.1 broadcast_in_dim.11
  52.0 0.0 copy-start.2
  52.0 359.2 %all-gather.2.cloned.1.call-done = f32[1024,4096]{1,0:T(8,128)} async-done(((f32[1024,128]{1,0:T(8,128)}), f32[1024,4096]{1,0:T(8,128)}) %all-gather.2.cloned.1.call-update) | async-done | bytes 16777232 | tf_op jit(solution)/shard_map/all_gather | solution.py:69
  411.2 0.0 copy-done.1
  411.2 13.9 %fusion = f32[2,16,4096]{2,1,0:T(8,128)} fusion(f32[1024,4096]{1,0:T(8,128)} %all-gather.2.cloned.1.call-done, f32[1,2,16,1024]{3,2,1,0:T(8,128)S(1)} %copy-done.1, f32[1,2,16,1024]{3,2,1,0:T(8,128)S(1)} %reshape.43), kind=kOutput, calls=%fused_computation | convolution fusion | flops 1610645504 | bytes 17563648 | tf_op jit(solution)/shard_map/lgrs,lsn->grn/dot_general | solution.py:56
  425.1 0.0 reduce-scatter.3.cloned.1.call-update
  425.2 0.0 all-reduce.6.cloned.1.call-start
  425.2 12.2 %reduce-scatter.3.cloned.1.call-done = f32[1,16,4096]{2,1,0:T(8,128)} async-done(((f32[2,16,4096]{2,1,0:T(8,128)}), f32[1,16,4096]{2,1,0:T(8,128)}) %reduce-scatter.3.cloned.1.call-update) | async-done | bytes 262160 | tf_op jit(solution)/shard_map/reduce_scatter | solution.py:19
  437.4 1.0 copy.21
  438.4 0.2 copy.17
  438.6 16.8 %all_to_all.35 = f32[16,32,128]{2,0,1:T(8,128)S(1)} all-to-all(f32[16,32,128]{2,0,1:T(8,128)S(1)} %copy.17), channel_id=1, replica_groups=mesh['depth'=2,'rows'=2,'shots'=32] {'shots'}, dimensions={1} | all-to-all | bytes 524288 | tf_op jit(solution)/shard_map/all_to_all | solution.py:64
  455.4 0.0 copy-done.2
  455.4 4.7 fusion.14
  460.1 0.0 all-reduce.6.cloned.1.call-update
  460.1 34.9 %all-reduce.6.cloned.1.call-done = f32[1024,128]{0,1:T(8,128)} async-done(((f32[1024,128]{0,1:T(8,128)}), f32[1024,128]{0,1:T(8,128)}) %all-reduce.6.cloned.1.call-update) | async-done | bytes 524304 | tf_op jit(solution)/shard_map/psum | solution.py:32
  494.9 3.1 fusion.2
  498.0 0.8 copy.18
  498.8 7.0 all-to-all-start.1
  505.8 0.0 reduce-scatter.5.cloned.1.call-start
  505.9 8.5 all-to-all-done.1
  514.4 0.1 copy.19
  514.5 0.1 broadcast_in_dim.12
  514.6 3.8 all_gather.7
  518.4 16.0 %convolution_bitcast_fusion = f32[1024,4096]{1,0:T(8,128)} fusion(f32[2,16,4096]{2,1,0:T(8,128)S(1)} %all_gather.7, f32[2,16,1024]{2,1,0:T(8,128)S(1)} %reshape.42, f32[1,2,16,1024]{3,2,1,0:T(8,128)S(1)} %copy-done.1), kind=kOutput, calls=%fused_computation.2 | convolution fusion | flops 1610645504 | bytes 17563648 | tf_op jit(solution)/shard_map/grs,grn->sn/dot_general | solution.py:76
  534.3 0.0 copy-start
  534.3 0.0 reduce-scatter.5.cloned.1.call-update
  534.3 0.0 all-reduce.8.cloned.1.call-start
  534.4 359.6 %reduce-scatter.5.cloned.1.call-done = f32[1024,128]{1,0:T(8,128)} async-done(((f32[1024,4096]{1,0:T(8,128)}), f32[1024,128]{1,0:T(8,128)}) %reduce-scatter.5.cloned.1.call-update) | async-done | bytes 524304 | tf_op jit(solution)/shard_map/reduce_scatter | solution.py:83
  894.0 0.0 all-reduce.8.cloned.1.call-update
  894.0 36.9 %all-reduce.8.cloned.1.call-done = f32[1024,128]{1,0:T(8,128)} async-done(((f32[1024,128]{1,0:T(8,128)}), f32[1024,128]{1,0:T(8,128)}) %all-reduce.8.cloned.1.call-update) | async-done | bytes 524304 | tf_op jit(solution)/shard_map/psum | solution.py:84
  930.9 0.0 copy-done
  930.9 3.2 fusion.17
  934.1 1.0 copy.20
  (4 shorter events, 0.1 us)
Async XLA Ops:
  6.5 404.7 %copy-start.1 = (f32[1,2,16,1024]{3,2,1,0:T(8,128)S(1)}, f32[1,2,16,1024]{3,2,1,0:T(8,128)}, u32[]{:S(2)}) copy-start(f32[1,2,16,1024]{3,2,1,0:T(8,128)} %param.5) | copy-start | bytes 393220
  6.5 44.3 %all-reduce.4.cloned.1.call-start = ((), (), s32[]{:S(2)}) async-start(), calls=%async_computation.4 | async-start | bytes 1048576 | tf_op jit(solution)/shard_map/psum | solution.py:32
  10.8 400.5 %all-gather.2.cloned.1.call-start = ((), (), s32[]{:S(2)}) async-start(), calls=%async_computation.5 | async-start | bytes 17301504 | tf_op jit(solution)/shard_map/all_gather | solution.py:69
  50.8 386.6 %reduce-scatter.3.cloned.1.call-start = ((), (), s32[]{:S(2)}) async-start(), calls=%async_computation.6 | async-start | bytes 786432 | tf_op jit(solution)/shard_map/reduce_scatter | solution.py:19
  52.0 403.4 %copy-start.2 = (f32[1,2,512,128]{3,2,1,0:T(8,128)S(1)}, f32[1,2,512,128]{3,2,1,0:T(8,128)}, u32[]{:S(2)}) copy-start(f32[1,2,512,128]{3,2,1,0:T(8,128)} %param.4) | copy-start | bytes 1572868
  425.2 69.8 %all-reduce.6.cloned.1.call-start = ((), (), s32[]{:S(2)}) async-start(), calls=%async_computation.7 | async-start | bytes 1048576 | tf_op jit(solution)/shard_map/psum | solution.py:32
  498.8 15.6 %all-to-all-start.1 = ((f32[32,16,128]{2,1,0:T(8,128)}), f32[32,16,128]{2,1,0:T(8,128)S(1)}, u32[]{:S(2)}, u32[]{:S(2)}) async-start(f32[32,16,128]{2,1,0:T(8,128)} %bitcast.16), calls=%async_computation.2 | async-start | bytes 524288 | tf_op jit(solution)/shard_map/all_to_all | solution.py:95
  505.8 388.2 %reduce-scatter.5.cloned.1.call-start = ((), (), s32[]{:S(2)}) async-start(), calls=%async_computation.8 | async-start | bytes 17301504 | tf_op jit(solution)/shard_map/reduce_scatter | solution.py:83
  534.3 396.6 %copy-start = (f32[1024,128]{1,0:T(8,128)S(1)}, f32[1024,128]{1,0:T(8,128)}, u32[]{:S(2)}) copy-start(f32[1024,128]{1,0:T(8,128)} %all-reduce.4.cloned.1.call-done) | copy-start | bytes 1572868
  534.3 396.6 %all-reduce.8.cloned.1.call-start = ((), (), s32[]{:S(2)}) async-start(), calls=%async_computation.9 | async-start | bytes 1048576 | tf_op jit(solution)/shard_map/psum | solution.py:84
Sparse Core Ops, SparseCore 0:
  10.9 39.8 all-reduce.3
  52.5 358.7 all-gather.1
  425.3 12.0 reduce-scatter.2
  460.2 34.6 all-reduce.5
  534.5 359.4 reduce-scatter.4
  896.5 34.4 all-reduce.7
where the time goes:
time: 942 us
  waiting for transfers between devices  851 us (90%)
  matrix products  45.1 us (5%)
  blocking collectives  20.6 us (2%)
  between operations  13.6 us (1%)
    reduce_scatter x1, waiting for transfers between devices, per_device(): lax.psum_scatter(transposed, 'shots', scatter_dimension=1, tiled=True)  360 us
    all_gather x1, waiting for transfers between devices, per_device(): wide_solved.append(lax.all_gather(full_rows, 'shots', axis=1, tiled=True))  359 us
    psum x2, waiting for transfers between devices, invert_level(): return lax.psum(inverse_term, 'rows')  74.8 us
    psum x1, waiting for transfers between devices, per_device(): own_columns = lax.psum(shot_piece, 'rows')  36.9 us
  transfers between devices with their start and end apart: 7, of which 7 were waited for; matrix products, arithmetic and copies ran while one was open for 0% of the time, Pallas kernels for 0%

commit v1 on v0

--- a/solution.py
+++ b/solution.py
@@ -81,7 +81,7 @@
                 preferred_element_type=jnp.float32,
             )
             shot_piece = lax.psum_scatter(transposed, "shots", scatter_dimension=1, tiled=True)
-            own_columns = lax.psum(shot_piece, "rows")
+            own_columns = jnp.sum(lax.all_gather(shot_piece, "rows"), axis=0)
             target = target - own_columns
         answer = lax.dot_general(
             inverse_diagonal[0, tier_index],

time: 942 us -> 931 us (0.988)
  waiting for transfers between devices: 851 us -> 839 us
    psum x1 -> x0, waiting for transfers between devices: 36.9 us -> none  [per_device(): own_columns = lax.psum(shot_piece, 'rows')]
    all_gather x0 -> x1, waiting for transfers between devices: none -> 24.7 us  [per_device(): own_columns = jnp.sum(lax.all_gather(shot_piece, 'rows'), axis=0)]
where the time goes in v1:
time: 931 us
  waiting for transfers between devices  839 us (90%)
  matrix products  44.9 us (5%)
  blocking collectives  20.6 us (2%)
  between operations  13.6 us (1%)
    reduce_scatter x1, waiting for transfers between devices, per_device(): lax.psum_scatter(transposed, 'shots', scatter_dimension=1, tiled=True)  360 us
    all_gather x1, waiting for transfers between devices, per_device(): wide_solved.append(lax.all_gather(full_rows, 'shots', axis=1, tiled=True))  359 us
    psum x2, waiting for transfers between devices, invert_level(): return lax.psum(inverse_term, 'rows')  74.8 us
    all_gather x1, waiting for transfers between devices, per_device(): own_columns = jnp.sum(lax.all_gather(shot_piece, 'rows'), axis=0)  24.7 us
  transfers between devices with their start and end apart: 7, of which 7 were waited for; matrix products, arithmetic and copies ran while one was open for 0% of the time, Pallas kernels for 0%

profile of v1, /device:TPU:1, one launch (start us, length us, event | category | flops | bytes accessed | tf_op | source)
XLA Modules:
  0.0 931.0 jit_solution(8326248717552514967)
XLA Ops:
  6.5 0.0 copy-start.1
  6.5 0.0 all-reduce.3.cloned.1.call-start
  6.5 4.2 fusion.8
  10.8 0.0 all-reduce.3.cloned.1.call-update
  10.8 0.0 all-gather.4.cloned.1.call-start
  10.8 40.0 %all-reduce.3.cloned.1.call-done = f32[1024,128]{1,0:T(8,128)} async-done(((f32[1024,128]{1,0:T(8,128)}), f32[1024,128]{1,0:T(8,128)}) %all-reduce.3.cloned.1.call-update) | async-done | bytes 524304 | tf_op jit(solution)/shard_map/psum | solution.py:32
  50.8 0.0 all-gather.4.cloned.1.call-update
  50.8 0.0 reduce-scatter.3.cloned.1.call-start
  50.9 0.7 convert_bitcast_fusion
  51.6 0.1 copy.21
  51.7 0.1 convolution_bitcast_fusion.1
  51.8 0.1 copy.22
  51.9 0.1 broadcast_in_dim.11
  52.0 0.0 copy-start.2
  52.0 359.2 %all-gather.4.cloned.1.call-done = f32[1024,4096]{1,0:T(8,128)} async-done(((f32[1024,128]{1,0:T(8,128)}), f32[1024,4096]{1,0:T(8,128)}) %all-gather.4.cloned.1.call-update) | async-done | bytes 16777232 | tf_op jit(solution)/shard_map/all_gather | solution.py:69
  411.2 0.0 copy-done.1
  411.2 13.9 %fusion = f32[2,16,4096]{2,1,0:T(8,128)} fusion(f32[1024,4096]{1,0:T(8,128)} %all-gather.4.cloned.1.call-done, f32[1,2,16,1024]{3,2,1,0:T(8,128)S(1)} %copy-done.1, f32[1,2,16,1024]{3,2,1,0:T(8,128)S(1)} %reshape.43), kind=kOutput, calls=%fused_computation | convolution fusion | flops 1610645504 | bytes 17563648 | tf_op jit(solution)/shard_map/lgrs,lsn->grn/dot_general | solution.py:56
  425.1 0.0 reduce-scatter.3.cloned.1.call-update
  425.2 0.0 all-reduce.5.cloned.1.call-start
  425.2 12.2 %reduce-scatter.3.cloned.1.call-done = f32[1,16,4096]{2,1,0:T(8,128)} async-done(((f32[2,16,4096]{2,1,0:T(8,128)}), f32[1,16,4096]{2,1,0:T(8,128)}) %reduce-scatter.3.cloned.1.call-update) | async-done | bytes 262160 | tf_op jit(solution)/shard_map/reduce_scatter | solution.py:19
  437.4 1.0 copy.27
  438.4 0.2 copy.23
  438.6 16.8 %all_to_all.35 = f32[16,32,128]{2,0,1:T(8,128)S(1)} all-to-all(f32[16,32,128]{2,0,1:T(8,128)S(1)} %copy.23), channel_id=1, replica_groups=mesh['depth'=2,'rows'=2,'shots'=32] {'shots'}, dimensions={1} | all-to-all | bytes 524288 | tf_op jit(solution)/shard_map/all_to_all | solution.py:64
  455.4 0.0 copy-done.2
  455.4 4.7 fusion.14
  460.1 0.0 all-reduce.5.cloned.1.call-update
  460.1 34.9 %all-reduce.5.cloned.1.call-done = f32[1024,128]{0,1:T(8,128)} async-done(((f32[1024,128]{0,1:T(8,128)}), f32[1024,128]{0,1:T(8,128)}) %all-reduce.5.cloned.1.call-update) | async-done | bytes 524304 | tf_op jit(solution)/shard_map/psum | solution.py:32
  494.9 3.1 fusion.2
  498.0 0.8 copy.24
  498.8 7.0 all-to-all-start.1
  505.8 0.0 reduce-scatter.5.cloned.1.call-start
  505.9 8.5 all-to-all-done.1
  514.4 0.1 copy.25
  514.5 0.1 broadcast_in_dim.12
  514.6 3.8 all_gather.13
  518.4 16.0 %convolution_bitcast_fusion = f32[1024,4096]{1,0:T(8,128)} fusion(f32[2,16,4096]{2,1,0:T(8,128)S(1)} %all_gather.13, f32[2,16,1024]{2,1,0:T(8,128)S(1)} %reshape.42, f32[1,2,16,1024]{3,2,1,0:T(8,128)S(1)} %copy-done.1), kind=kOutput, calls=%fused_computation.2 | convolution fusion | flops 1610645504 | bytes 17563648 | tf_op jit(solution)/shard_map/grs,grn->sn/dot_general | solution.py:76
  534.3 0.0 copy-start
  534.3 0.0 reduce-scatter.5.cloned.1.call-update
  534.3 0.0 all-gather.6.cloned.1.call-start
  534.4 359.6 %reduce-scatter.5.cloned.1.call-done = f32[1024,128]{1,0:T(8,128)} async-done(((f32[1024,4096]{1,0:T(8,128)}), f32[1024,128]{1,0:T(8,128)}) %reduce-scatter.5.cloned.1.call-update) | async-done | bytes 524304 | tf_op jit(solution)/shard_map/reduce_scatter | solution.py:83
  894.0 0.0 all-gather.6.cloned.1.call-update
  894.0 24.7 %all-gather.6.cloned.1.call-done = f32[2048,128]{1,0:T(8,128)} async-done(((f32[1024,128]{1,0:T(8,128)}), f32[2048,128]{1,0:T(8,128)}) %all-gather.6.cloned.1.call-update) | async-done | bytes 1048592 | tf_op jit(solution)/shard_map/all_gather | solution.py:84
  918.7 1.3 reduce_sum.9
  920.1 0.0 copy-done
  920.1 3.0 fusion.17
  923.1 1.0 copy.26
  (4 shorter events, 0.1 us)
Async XLA Ops:
  6.5 404.7 %copy-start.1 = (f32[1,2,16,1024]{3,2,1,0:T(8,128)S(1)}, f32[1,2,16,1024]{3,2,1,0:T(8,128)}, u32[]{:S(2)}) copy-start(f32[1,2,16,1024]{3,2,1,0:T(8,128)} %param.5) | copy-start | bytes 393220
  6.5 44.3 %all-reduce.3.cloned.1.call-start = ((), (), s32[]{:S(2)}) async-start(), calls=%async_computation.4 | async-start | bytes 1048576 | tf_op jit(solution)/shard_map/psum | solution.py:32
  10.8 400.5 %all-gather.4.cloned.1.call-start = ((), (), s32[]{:S(2)}) async-start(), calls=%async_computation.5 | async-start | bytes 17301504 | tf_op jit(solution)/shard_map/all_gather | solution.py:69
  50.8 386.6 %reduce-scatter.3.cloned.1.call-start = ((), (), s32[]{:S(2)}) async-start(), calls=%async_computation.6 | async-start | bytes 786432 | tf_op jit(solution)/shard_map/reduce_scatter | solution.py:19
  52.0 403.4 %copy-start.2 = (f32[1,2,512,128]{3,2,1,0:T(8,128)S(1)}, f32[1,2,512,128]{3,2,1,0:T(8,128)}, u32[]{:S(2)}) copy-start(f32[1,2,512,128]{3,2,1,0:T(8,128)} %param.4) | copy-start | bytes 1572868
  425.2 69.8 %all-reduce.5.cloned.1.call-start = ((), (), s32[]{:S(2)}) async-start(), calls=%async_computation.7 | async-start | bytes 1048576 | tf_op jit(solution)/shard_map/psum | solution.py:32
  498.8 15.6 %all-to-all-start.1 = ((f32[32,16,128]{2,1,0:T(8,128)}), f32[32,16,128]{2,1,0:T(8,128)S(1)}, u32[]{:S(2)}, u32[]{:S(2)}) async-start(f32[32,16,128]{2,1,0:T(8,128)} %bitcast.16), calls=%async_computation.2 | async-start | bytes 524288 | tf_op jit(solution)/shard_map/all_to_all | solution.py:95
  505.8 388.2 %reduce-scatter.5.cloned.1.call-start = ((), (), s32[]{:S(2)}) async-start(), calls=%async_computation.8 | async-start | bytes 17301504 | tf_op jit(solution)/shard_map/reduce_scatter | solution.py:83
  534.3 385.8 %copy-start = (f32[1024,128]{1,0:T(8,128)S(1)}, f32[1024,128]{1,0:T(8,128)}, u32[]{:S(2)}) copy-start(f32[1024,128]{1,0:T(8,128)} %all-reduce.3.cloned.1.call-done) | copy-start | bytes 1572868
  534.3 384.4 %all-gather.6.cloned.1.call-start = ((), (), s32[]{:S(2)}) async-start(), calls=%async_computation.9 | async-start | bytes 1572864 | tf_op jit(solution)/shard_map/all_gather | solution.py:84
Sparse Core Ops, SparseCore 0:
  10.9 39.8 all-reduce.2
  52.5 358.7 all-gather.3
  425.3 12.0 reduce-scatter.2
  460.2 34.6 all-reduce.4
  534.5 359.4 reduce-scatter.4
  895.6 23.0 all-gather.5
